TPU v7x, 256 devices: a whole 4x4x8 slice. The times are simulated.
256 devices in a mesh: ctx: 64 (over z, x, core), dp: 4 (over y).
Axes of the slice: x: 4, y: 4, z: 8, core: 2. Of those that a mesh axis runs over, the one named last changes fastest.
Arguments:
- query_in: bfloat16 [4, 16384, 4096], P('dp', 'ctx'), may hold values from -6 to 6
- key_in: bfloat16 [4, 16384, 512], P('dp', 'ctx'), may hold values from -6 to 6
- value_rows_input: bfloat16 [4, 16384, 512], P('dp', 'ctx'), may hold values from -6 to 6
- grad_out: bfloat16 [4, 16384, 4096], P('dp', 'ctx'), may hold values from -12 to 12
- query_bias: float32 [4096], replicated, may hold values from -1.5 to 1.5
- key_blocks: int32 [4, 128, 6], P('dp'), may hold values from -1 to 127, as said below
- trace_len: int32 [4], P('dp'), may hold values from 8192 to 16384, as said below
Outputs:
- grad_query: bfloat16 [4, 16384, 4096], P('dp', 'ctx')
- grad_key: bfloat16 [4, 16384, 512], P('dp', 'ctx')
- grad_value: bfloat16 [4, 16384, 512], P('dp', 'ctx')
- bias_grad: float32 [4096], replicated
Inputs may be any that keep to these rules, and one draw needn't show every extreme that they name: `key_blocks`: blocks are numbered by position. Entry 2 + d of query block q's list is q - d or -1, and entry 2 is always q; entry r < 2 is r or -1, and -1 whenever r >= q - 3. `trace_len`: some trace has 16384 tokens and some 16384 // 2.
All inputs are finite; a program needn't handle non-finite values.
Results may differ from a plain program's by a relative error of at most 0.011.
The roundings to bfloat16 on the way count: a program that leaves them out, or rounds other values in their place, can miss the bound.
Values may be sent and summed in bfloat16 or wider, within the bound.
A program may use at most 128 MiB of HBM per device.

v0:
```python
import math
import jax
import jax.numpy as jnp
from jax import lax
from jax.sharding import PartitionSpec as P

HEAD_SIZE = 128
BLOCK = 128
PROMPT = 2
WINDOW = 3


def from_behind(value, axis, steps):
    count = lax.axis_size(axis)
    initial, last = (max(0, -steps), min(count, count - steps))
    return lax.ppermute(value, axis, [(source, source + steps) for source in range(initial, last)])


def broadcast(value, axis, source):
    kept = jnp.where(lax.axis_index(axis) == source, value, 0).astype(value.dtype)
    return lax.psum(kept, axis)


def attend(queries, cand_keys, cand_vals, grad_rows, allowed):
    score_scale = HEAD_SIZE ** (-0.5)
    scores = score_scale * jnp.einsum(
        "tqkgd,tskd->tkgqs", queries, cand_keys, preferred_element_type=jnp.float32
    )
    mask_full = allowed[:, None, None]
    scores = jnp.where(mask_full, scores, -1e30)
    row_max = jnp.max(scores, axis=-1, keepdims=True)
    probs = jnp.where(mask_full, jnp.exp(scores - row_max), 0.0)
    totals = jnp.sum(probs, axis=-1, keepdims=True)
    row_live = jnp.any(allowed, axis=-1)[:, None, None, :, None]
    probs = probs / jnp.where(row_live, totals, 1.0)
    probs_low = probs.astype(jnp.bfloat16)
    attended = jnp.einsum(
        "tkgqs,tskd->tqkgd", probs_low, cand_vals, preferred_element_type=jnp.float32
    )
    row_dot = jnp.sum(grad_rows * attended, axis=-1).transpose(0, 2, 3, 1)[..., None]
    grad_probs = jnp.einsum(
        "tqkgd,tskd->tkgqs", grad_rows, cand_vals, preferred_element_type=jnp.float32
    )
    grad_scores = (probs * (grad_probs - row_dot)).astype(jnp.bfloat16)
    grad_query = score_scale * jnp.einsum(
        "tkgqs,tskd->tqkgd", grad_scores, cand_keys, preferred_element_type=jnp.float32
    )
    grad_key = score_scale * jnp.einsum(
        "tkgqs,tqkgd->tskd", grad_scores, queries, preferred_element_type=jnp.float32
    )
    grad_value = jnp.einsum(
        "tkgqs,tqkgd->tskd", probs_low, grad_rows, preferred_element_type=jnp.float32
    )
    return (grad_query, grad_key, grad_value)


def body(query_in, key_in, value_rows_input, grad_out, query_bias, key_blocks, trace_len):
    ctx_count = lax.axis_size("ctx")
    rank_ctx = lax.axis_index("ctx")
    traces = query_in.shape[0]
    width_kv = key_in.shape[-1]
    width_q = query_in.shape[-1]
    heads_kv = width_kv // HEAD_SIZE
    group_size = width_q // width_kv
    cand_count = PROMPT + WINDOW + 1
    kv_pair = jnp.concatenate([key_in, value_rows_input], axis=-1).reshape(
        traces, 2, BLOCK, 2 * width_kv
    )
    own_ids = jnp.stack([rank_ctx, 2 * ctx_count - 1 - rank_ctx])
    half_count = kv_pair.shape[1]
    from_lower = jnp.stack([from_behind(kv_pair, "ctx", offset) for offset in range(1, WINDOW + 1)])
    from_upper = jnp.stack(
        [from_behind(kv_pair, "ctx", -offset) for offset in range(1, WINDOW + 1)]
    )
    offsets = jnp.arange(1, WINDOW + 1, dtype=jnp.int32)
    lower_dev = rank_ctx - offsets
    upper_dev = rank_ctx + offsets
    lower_ids = jnp.stack([lower_dev, 2 * ctx_count - 1 - lower_dev], axis=1)
    upper_ids = jnp.stack([upper_dev, 2 * ctx_count - 1 - upper_dev], axis=1)
    lower_ids = jnp.where((lower_dev >= 0)[:, None], lower_ids, -1000).reshape(-1)
    upper_ids = jnp.where((upper_dev < ctx_count)[:, None], upper_ids, -1000).reshape(-1)
    lower_data = from_lower.transpose(1, 0, 2, 3, 4).reshape(
        traces, WINDOW * half_count, BLOCK, 2 * width_kv
    )
    upper_data = from_upper.transpose(1, 0, 2, 3, 4).reshape(
        traces, WINDOW * half_count, BLOCK, 2 * width_kv
    )
    data_list = [kv_pair, lower_data, upper_data]
    id_list = [own_ids, lower_ids, upper_ids]
    slot_data = jnp.concatenate(data_list, axis=1)
    slot_ids = jnp.concatenate(id_list)
    targets = own_ids[:, None] - jnp.arange(WINDOW + 1, dtype=jnp.int32)[None]
    chooser = (slot_ids[None, None, :] == targets[..., None]).astype(jnp.bfloat16)
    window_kv = jnp.einsum(
        "jdn,tnbf->tjdbf", chooser, slot_data, preferred_element_type=jnp.float32
    ).astype(jnp.bfloat16)
    first_half = kv_pair[:, 0]
    prompt_kv = jnp.stack(
        [broadcast(first_half, "ctx", source) for source in range(PROMPT)], axis=1
    )
    block_rows = jnp.take(key_blocks, own_ids, axis=1)
    queries = (
        (query_in.astype(jnp.float32) + query_bias)
        .astype(jnp.bfloat16)
        .reshape(traces, 2, BLOCK, heads_kv, group_size, HEAD_SIZE)
    )
    grad_rows = grad_out.reshape(traces, 2, BLOCK, heads_kv, group_size, HEAD_SIZE)
    prompt_grad = jnp.zeros((traces, PROMPT, BLOCK, 2 * width_kv), jnp.float32)
    slot_grad = jnp.zeros((traces, slot_data.shape[1], BLOCK, 2 * width_kv), jnp.float32)
    query_parts = []
    for half_idx in range(2):
        block_here = own_ids[half_idx]
        candidates = jnp.concatenate([prompt_kv, window_kv[:, half_idx]], axis=1)
        cand_keys = candidates[..., :width_kv].reshape(
            traces, cand_count * BLOCK, heads_kv, HEAD_SIZE
        )
        cand_vals = candidates[..., width_kv:].reshape(
            traces, cand_count * BLOCK, heads_kv, HEAD_SIZE
        )
        key_ids = jnp.concatenate(
            [
                jnp.arange(PROMPT, dtype=jnp.int32),
                block_here - jnp.arange(WINDOW + 1, dtype=jnp.int32),
            ]
        )
        prompt_ok = jnp.concatenate(
            [
                jnp.arange(PROMPT, dtype=jnp.int32) < block_here - WINDOW,
                jnp.ones((WINDOW + 1,), jnp.bool_),
            ]
        )
        block_ok = (block_rows[:, half_idx] >= 0) & prompt_ok[None]
        key_pos = (key_ids[:, None] * BLOCK + jnp.arange(BLOCK, dtype=jnp.int32)[None]).reshape(-1)
        query_pos = block_here * BLOCK + jnp.arange(BLOCK, dtype=jnp.int32)
        length = trace_len[:, None, None]
        allowed = (
            jnp.repeat(block_ok, BLOCK, axis=1)[:, None, :]
            & (key_pos[None, None, :] <= query_pos[None, :, None])
            & (key_pos[None, None, :] < length)
            & (query_pos[None, :, None] < length)
        )
        grad_query, grad_key, grad_value = attend(
            queries[:, half_idx], cand_keys, cand_vals, grad_rows[:, half_idx], allowed
        )
        query_parts.append(grad_query)
        contrib = jnp.concatenate(
            [
                grad_key.reshape(traces, cand_count, BLOCK, width_kv),
                grad_value.reshape(traces, cand_count, BLOCK, width_kv),
            ],
            axis=-1,
        )
        prompt_grad = prompt_grad + contrib[:, :PROMPT]
        slot_grad = slot_grad + jnp.einsum(
            "dn,tdbf->tnbf",
            chooser[half_idx].astype(jnp.float32),
            contrib[:, PROMPT:],
            precision=lax.Precision.HIGHEST,
        )
    span = WINDOW * half_count
    own_grad = slot_grad[:, 0:2]
    lower_grad = (
        slot_grad[:, 2 : 2 + span]
        .reshape(traces, WINDOW, half_count, BLOCK, 2 * width_kv)
        .transpose(1, 0, 2, 3, 4)
    )
    upper_grad = (
        slot_grad[:, 2 + span : 2 + 2 * span]
        .reshape(traces, WINDOW, half_count, BLOCK, 2 * width_kv)
        .transpose(1, 0, 2, 3, 4)
    )
    low_part = jnp.zeros_like(lower_grad[0])
    up_part = jnp.zeros_like(upper_grad[0])
    for offset in range(1, WINDOW + 1):
        low_part = low_part + from_behind(lower_grad[offset - 1], "ctx", -offset)
        up_part = up_part + from_behind(upper_grad[offset - 1], "ctx", offset)
    kv_grad = own_grad + low_part + up_part
    owners = jnp.arange(PROMPT, dtype=jnp.int32)
    query_all = jnp.stack(query_parts, axis=1)
    local_bias = jnp.sum(query_all, axis=(0, 1, 2)).reshape(width_q)
    shared_total = lax.psum(prompt_grad, "ctx")
    bias_total = lax.psum(local_bias, ("ctx", "dp"))
    owned = (owners == rank_ctx).astype(jnp.float32)
    kv_grad = kv_grad.at[:, 0].add(jnp.sum(owned[None, :, None, None] * shared_total, axis=1))
    grad_query_out = query_all.reshape(traces, 2 * BLOCK, width_q).astype(jnp.bfloat16)
    grad_key_out = kv_grad[..., :width_kv].reshape(traces, 2 * BLOCK, width_kv).astype(jnp.bfloat16)
    grad_value_out = (
        kv_grad[..., width_kv:].reshape(traces, 2 * BLOCK, width_kv).astype(jnp.bfloat16)
    )
    all_traces = traces * lax.axis_size("dp")
    bias_out = bias_total / math.sqrt(all_traces * 2 * BLOCK * ctx_count)
    return (grad_query_out, grad_key_out, grad_value_out, bias_out)


def solution(mesh):
    return jax.shard_map(
        body,
        mesh=mesh,
        in_specs=(
            P("dp", "ctx", None),
            P("dp", "ctx", None),
            P("dp", "ctx", None),
            P("dp", "ctx", None),
            P(),
            P("dp", None, None),
            P("dp"),
        ),
        out_specs=(P("dp", "ctx", None), P("dp", "ctx", None), P("dp", "ctx", None), P()),
        check_vma=False,
    )
```

profile of v0, /device:TPU:2, one launch (start us, length us, event | category | flops | bytes accessed | tf_op | source)
XLA Modules:
  0.0 588.3 jit_solution(5824512596889643687)
XLA Ops:
  9.7 4.2 collective-permute-start.4
  15.9 4.8 collective-permute-start.2
  35.2 2.9 fusion.73
  38.3 3.7 collective-permute-start
  42.5 3.3 fusion.74
  48.9 4.4 collective-permute-done
  55.6 2.7 convert_bitcast_fusion
  60.0 162.5 %all-reduce.8.cloned.1.call-done = (bf16[1,1,128,1024]{3,1,2,0:T(2,128)(2,1)}, bf16[1,1,128,1024]{3,1,2,0:T(2,128)(2,1)}) async-done(((bf16[1,1,128,1024]{3,1,2,0:T(2,128)(2,1)}, bf16[1,1,128,1024]{3,1,2,0:T(2,128)(2,1)}), (bf16[1,1,128,1024]{3,1,2,0:T(2,128)(2,1)}, bf16[1,1,128,1024]{3,1,2,0:T(2,128)(2,1)})) %all-reduce.8.cloned.1.call-update) | async-done | bytes 524304 | tf_op jit(solution)/shard_map/psum | solution.py:21
  222.5 4.6 pad_maximum_fusion
  233.5 2.7 fusion.75
  248.8 3.2 fusion.9
  252.0 5.3 fusion.40
  257.4 5.2 fusion.29
  262.6 7.1 %fusion.11 = bf16[4,8,128,768]{2,3,1,0:T(8,128)(2,1)S(1)} fusion(f32[4,8,128]{2,1,0:T(8,128)S(1)} %bitcast.338, f32[4,8,128]{2,1,0:T(8,128)S(1)} %broadcast_select_fusion.2, f32[4,8,128]{2,1,0:T(8,128)S(1)} %get-tuple-element.46, f32[4,768,128,8]{2,1,3,0:T(8,128)S(1)} %get-tuple-element.47, pred[128,768]{0,1:T(8,128)(4,1)S(1)} %and_and_fusion, ...), kind=kOutput, calls=%fused_computation.19 | convolution fusion | flops 830472192 | bytes 20856832 | tf_op jit(solution)/shard_map/tqkgd,tskd->tkgqs/dot_general | solution.py:41
  272.8 3.4 fusion.35
  276.2 2.8 copy.106
  279.0 3.7 copy_dynamic-update-slice_fusion.1
  285.1 3.2 fusion.7
  288.4 4.8 fusion.37
  293.2 5.2 fusion.30
  298.4 7.3 %fusion.10 = bf16[4,8,128,768]{2,3,1,0:T(8,128)(2,1)S(1)} fusion(f32[4,8,128]{2,1,0:T(8,128)S(1)} %bitcast.339, f32[4,8,128]{2,1,0:T(8,128)S(1)} %broadcast_select_fusion.3, f32[4,8,128]{2,1,0:T(8,128)S(1)} %get-tuple-element.48, f32[4,768,128,8]{2,1,3,0:T(8,128)S(1)} %get-tuple-element.49, pred[128,768]{0,1:T(8,128)(4,1)S(1)} %and_and_fusion.1, ...), kind=kOutput, calls=%fused_computation.18 | convolution fusion | flops 830472192 | bytes 20856832 | tf_op jit(solution)/shard_map/tqkgd,tskd->tkgqs/dot_general | solution.py:41
  308.8 3.4 fusion.36
  318.2 6.9 %fusion.28 = f32[128,1024,14]{1,2,0:T(8,128)} fusion(f32[1,6,128,1024]{3,1,2,0:T(8,128)S(1)} %copy_dynamic-update-slice_fusion.2, pred[2,4,14]{2,1,0:T(4,128)(4,1)S(1)} %copy-done.26), kind=kOutput, calls=%fused_computation.40 | convolution fusion | flops 88080384 | bytes 9437696 | tf_op jit(solution)/shard_map/dn,tdbf->tnbf/dot_general | solution.py:154
  330.1 10.6 %add_bitcast_fusion = f32[1,14,128,1024]{3,1,2,0:T(8,128)S(1)} fusion(f32[128,1024,14]{1,2,0:T(8,128)} %fusion.28, f32[1,6,128,1024]{3,1,2,0:T(8,128)} %copy-done.4, pred[2,4,14]{2,1,0:T(4,128)(4,1)S(1)} %copy-done.26), kind=kOutput, calls=%fused_computation.17 | convolution fusion | flops 89915392 | bytes 17826304 | tf_op jit(solution)/shard_map/dn,tdbf->tnbf/dot_general | solution.py:154
  340.8 3.6 fusion.71
  350.4 3.0 collective-permute-start.10
  353.4 4.5 collective-permute-start.9
  365.1 23.8 %collective-permute-done.7 = f32[1,2,128,1024]{3,1,2,0:T(2,128)S(1)} collective-permute-done((f32[1,2,128,1024]{3,1,2,0:T(2,128)S(1)}, f32[1,2,128,1024]{3,1,2,0:T(2,128)S(1)}, u32[]{:S(2)}, u32[]{:S(2)}) %collective-permute-start.7) | collective-permute-done | bytes 1048608 | tf_op jit(solution)/shard_map/ppermute | solution.py:16
  395.0 95.3 %psum.31 = f32[4096]{0:T(1024)S(1)} all-reduce(f32[4096]{0:T(1024)S(1)} %add_bitcast_fusion.1), channel_id=1, replica_groups=mesh['ctx'=64,'dp'=4] {'ctx','dp'}, use_global_device_ids=true, to_apply=%region_14.15 | all-reduce | flops 4096 | bytes 32768 | tf_op jit(solution)/shard_map/psum | solution.py:182
  490.9 75.6 %all-reduce.6.cloned.1.call-done = f32[1,2,128,1024]{3,1,2,0:T(2,128)} async-done(((f32[1,2,128,1024]{3,1,2,0:T(2,128)}), f32[1,2,128,1024]{3,1,2,0:T(2,128)}) %all-reduce.6.cloned.1.call-update) | async-done | bytes 1048592 | tf_op jit(solution)/shard_map/psum | solution.py:181
  569.2 5.6 fusion.45
  575.4 3.7 scatter-add.4
  (170 shorter events, 89.5 us)
Async XLA Ops:
  7.2 20.2 %copy-start.13 = (bf16[1,256,4096]{2,1,0:T(8,128)(2,1)S(1)}, bf16[1,256,4096]{2,1,0:T(8,128)(2,1)}, u32[]{:S(2)}) copy-start(bf16[1,256,4096]{2,1,0:T(8,128)(2,1)} %param.9) | copy-start | bytes 6291460
  7.2 215.4 %all-reduce.8.cloned.1.call-start = ((), (), s32[]{:S(2)}) async-start(), calls=%async_computation.1 | async-start | bytes 2097152 | tf_op jit(solution)/shard_map/psum | solution.py:21
  8.4 29.9 %collective-permute-start.5 = (bf16[1,2,128,1024]{3,2,1,0:T(8,128)(2,1)S(1)}, bf16[1,2,128,1024]{3,2,1,0:T(8,128)(2,1)}, u32[]{:S(2)}, u32[]{:S(2)}) collective-permute-start(bf16[1,2,128,1024]{3,2,1,0:T(8,128)(2,1)S(1)} %bitcast.327), channel_id=1, source_target_pairs={{12,0},{16,4},{20,8},{24,12},{28,16},{32,20},{36,24},{40,28},{44,3... | collective-permute-start | bytes 1572872 | tf_op jit(solution)/shard_map/ppermute | solution.py:16
  9.7 36.0 %collective-permute-start.4 = (bf16[1,2,128,1024]{3,2,1,0:T(8,128)(2,1)S(1)}, bf16[1,2,128,1024]{3,2,1,0:T(8,128)(2,1)}, u32[]{:S(2)}, u32[]{:S(2)}) collective-permute-start(bf16[1,2,128,1024]{3,2,1,0:T(8,128)(2,1)S(1)} %bitcast.328), channel_id=1, source_target_pairs={{8,0},{12,4},{16,8},{20,12},{24,16},{28,20},{32,24},{36,28},{40,32... | collective-permute-start | bytes 1572872 | tf_op jit(solution)/shard_map/ppermute | solution.py:16
  13.9 31.8 %collective-permute-start.3 = (bf16[1,2,128,1024]{3,2,1,0:T(8,128)(2,1)S(1)}, bf16[1,2,128,1024]{3,2,1,0:T(8,128)(2,1)}, u32[]{:S(2)}, u32[]{:S(2)}) collective-permute-start(bf16[1,2,128,1024]{3,2,1,0:T(8,128)(2,1)S(1)} %bitcast.329), channel_id=1, source_target_pairs={{4,0},{8,4},{12,8},{16,12},{20,16},{24,20},{28,24},{32,28},{36,32}... | collective-permute-start | bytes 1572872 | tf_op jit(solution)/shard_map/ppermute | solution.py:16
  15.9 32.3 %collective-permute-start.2 = (bf16[1,2,128,1024]{3,2,1,0:T(8,128)(2,1)S(1)}, bf16[1,2,128,1024]{3,2,1,0:T(8,128)(2,1)}, u32[]{:S(2)}, u32[]{:S(2)}) collective-permute-start(bf16[1,2,128,1024]{3,2,1,0:T(8,128)(2,1)S(1)} %bitcast.330), channel_id=1, source_target_pairs={{0,12},{4,16},{8,20},{12,24},{16,28},{20,32},{24,36},{28,40},{32,4... | collective-permute-start | bytes 1572872 | tf_op jit(solution)/shard_map/ppermute | solution.py:16
  20.7 28.1 %collective-permute-start.1 = (bf16[1,2,128,1024]{3,2,1,0:T(8,128)(2,1)S(1)}, bf16[1,2,128,1024]{3,2,1,0:T(8,128)(2,1)}, u32[]{:S(2)}, u32[]{:S(2)}) collective-permute-start(bf16[1,2,128,1024]{3,2,1,0:T(8,128)(2,1)S(1)} %bitcast.331), channel_id=1, source_target_pairs={{0,8},{4,12},{8,16},{12,20},{16,24},{20,28},{24,32},{28,36},{32,40... | collective-permute-start | bytes 1572872 | tf_op jit(solution)/shard_map/ppermute | solution.py:16
  25.0 541.6 %all-reduce.6.cloned.1.call-start = ((), (), s32[]{:S(2)}) async-start(), calls=%async_computation | async-start | bytes 2097152 | tf_op jit(solution)/shard_map/psum | solution.py:181
  32.8 22.8 %copy-start.25 = (pred[2,4,14]{2,1,0:T(4,128)(4,1)}, pred[2,4,14]{2,1,0:T(4,128)(4,1)S(1)}, u32[]{:S(2)}) copy-start(pred[2,4,14]{2,1,0:T(4,128)(4,1)S(1)} %broadcast_compare_fusion.2) | copy-start | bytes 340
  38.1 208.3 %copy-start.9 = (bf16[1,1,128,4,8,128]{5,4,3,2,1,0:T(8,128)(2,1)}, bf16[1,1,128,4,8,128]{5,4,3,2,1,0:T(8,128)(2,1)S(1)}, u32[]{:S(2)}) copy-start(bf16[1,1,128,4,8,128]{5,4,3,2,1,0:T(8,128)(2,1)S(1)} %get-tuple-element.29) | copy-start | bytes 3145732
  38.3 15.0 %collective-permute-start = (bf16[1,2,128,1024]{3,2,1,0:T(8,128)(2,1)S(1)}, bf16[1,2,128,1024]{3,2,1,0:T(8,128)(2,1)S(1)}, u32[]{:S(2)}, u32[]{:S(2)}) collective-permute-start(bf16[1,2,128,1024]{3,2,1,0:T(8,128)(2,1)S(1)} %bitcast.333), channel_id=1, source_target_pairs={{0,4},{4,8},{8,12},{12,16},{16,20},{20,24},{24,28},{28,32},{32,36}... | collective-permute-start | bytes 1572872 | tf_op jit(solution)/shard_map/ppermute | solution.py:16
  239.1 9.7 %copy-start.5 = (bf16[768,4,128]{2,1,0:T(4,128)(2,1)}, bf16[768,4,128]{2,1,0:T(4,128)(2,1)S(1)}, u32[]{:S(2)}) copy-start(bf16[768,4,128]{2,1,0:T(4,128)(2,1)S(1)} %reshape.1055) | copy-start | bytes 2359300
  252.0 5.3 copy-start.24
  262.6 7.1 %copy-start.15 = (f32[1,768,4,128]{3,1,2,0:T(8,128)S(1)}, f32[1,768,4,128]{3,1,2,0:T(8,128)}, u32[]{:S(2)}) copy-start(f32[1,768,4,128]{3,1,2,0:T(8,128)} %fusion.40) | copy-start | bytes 4718596
  262.6 10.2 %copy-start.10 = (bf16[1,1,128,4,8,128]{5,4,3,2,1,0:T(8,128)(2,1)S(1)}, bf16[1,1,128,4,8,128]{5,4,3,2,1,0:T(8,128)(2,1)}, u32[]{:S(2)}) copy-start(bf16[1,1,128,4,8,128]{5,4,3,2,1,0:T(8,128)(2,1)} %copy-done.9) | copy-start | bytes 3145732
  276.2 6.6 %copy-start.7 = (bf16[1,1,128,4,8,128]{5,4,3,2,1,0:T(8,128)(2,1)S(1)}, bf16[1,1,128,4,8,128]{5,4,3,2,1,0:T(8,128)(2,1)}, u32[]{:S(2)}) copy-start(bf16[1,1,128,4,8,128]{5,4,3,2,1,0:T(8,128)(2,1)} %get-tuple-element.28) | copy-start | bytes 3145732
  298.3 7.3 %copy-start.16 = (f32[1,768,4,128]{3,1,2,0:T(8,128)S(1)}, f32[1,768,4,128]{3,1,2,0:T(8,128)}, u32[]{:S(2)}) copy-start(f32[1,768,4,128]{3,1,2,0:T(8,128)} %fusion.37) | copy-start | bytes 4718596
  298.4 10.5 %copy-start.8 = (bf16[1,1,128,4,8,128]{5,4,3,2,1,0:T(8,128)(2,1)S(1)}, bf16[1,1,128,4,8,128]{5,4,3,2,1,0:T(8,128)(2,1)}, u32[]{:S(2)}) copy-start(bf16[1,1,128,4,8,128]{5,4,3,2,1,0:T(8,128)(2,1)} %get-tuple-element.28) | copy-start | bytes 3145732
  312.2 6.0 %copy-start.26 = (pred[2,4,14]{2,1,0:T(4,128)(4,1)S(1)}, pred[2,4,14]{2,1,0:T(4,128)(4,1)}, u32[]{:S(2)}) copy-start(pred[2,4,14]{2,1,0:T(4,128)(4,1)} %copy-done.25) | copy-start | bytes 340
  318.2 6.9 %copy-start.3 = (f32[1,6,128,1024]{3,1,2,0:T(8,128)S(1)}, f32[1,6,128,1024]{3,1,2,0:T(8,128)}, u32[]{:S(2)}) copy-start(f32[1,6,128,1024]{3,1,2,0:T(8,128)} %copy_dynamic-update-slice_fusion.1) | copy-start | bytes 9437188
  318.2 6.9 %copy-start.11 = (f32[1,768,4,128]{3,2,0,1:T(4,128)S(1)}, f32[1,768,4,128]{3,2,0,1:T(4,128)}, u32[]{:S(2)}) copy-start(f32[1,768,4,128]{3,2,0,1:T(4,128)} %copy.107) | copy-start | bytes 4718596
  328.1 31.9 %slice-start = ((s8[6291456]{0:T(1024)(128)(4,1)}), s8[2097152]{0:T(1024)(128)(4,1)S(1)}, s32[]{:S(2)}) async-start(s8[6291456]{0:T(1024)(128)(4,1)} %bitcast.308), calls=%async_computation.2 | async-start | bytes 4194304
  330.1 29.8 %slice-start.1 = ((s8[6291456]{0:T(1024)(128)(4,1)}), s8[4194304]{0:T(1024)(128)(4,1)S(1)}, s32[]{:S(2)}) async-start(s8[6291456]{0:T(1024)(128)(4,1)} %bitcast.308), calls=%async_computation.3 | async-start | bytes 8388608
  340.8 19.2 %copy-start.6 = (bf16[768,4,128]{2,1,0:T(4,128)(2,1)S(1)}, bf16[768,4,128]{2,1,0:T(4,128)(2,1)}, u32[]{:S(2)}) copy-start(bf16[768,4,128]{2,1,0:T(4,128)(2,1)} %copy-done.5) | copy-start | bytes 2359300
  345.6 43.2 %collective-permute-start.7 = (f32[1,2,128,1024]{3,1,2,0:T(2,128)S(1)}, f32[1,2,128,1024]{3,1,2,0:T(2,128)S(1)}, u32[]{:S(2)}, u32[]{:S(2)}) collective-permute-start(f32[1,2,128,1024]{3,1,2,0:T(2,128)S(1)} %get-tuple-element.20), channel_id=1, source_target_pairs={{8,0},{12,4},{16,8},{20,12},{24,16},{28,20},{32,24},{36,28},{40,32... | collective-permute-start | bytes 3145736 | tf_op jit(solution)/shard_map/ppermute | solution.py:16
  348.1 221.1 %collective-permute-start.11 = (f32[1,2,128,1024]{3,1,2,0:T(2,128)}, f32[1,2,128,1024]{3,1,2,0:T(2,128)}, u32[]{:S(2)}, u32[]{:S(2)}) collective-permute-start(f32[1,2,128,1024]{3,1,2,0:T(2,128)} %get-tuple-element.21), channel_id=1, source_target_pairs={{0,12},{4,16},{8,20},{12,24},{16,28},{20,32},{24,36},{28,40},{32,4... | collective-permute-start | bytes 3145736 | tf_op jit(solution)/shard_map/ppermute | solution.py:16
  350.4 218.7 %collective-permute-start.10 = (f32[1,2,128,1024]{3,1,2,0:T(2,128)}, f32[1,2,128,1024]{3,1,2,0:T(2,128)}, u32[]{:S(2)}, u32[]{:S(2)}) collective-permute-start(f32[1,2,128,1024]{3,1,2,0:T(2,128)} %get-tuple-element.22), channel_id=1, source_target_pairs={{0,8},{4,12},{8,16},{12,20},{16,24},{20,28},{24,32},{28,36},{32,40... | collective-permute-start | bytes 3145736 | tf_op jit(solution)/shard_map/ppermute | solution.py:16
  353.4 215.8 %collective-permute-start.9 = (f32[1,2,128,1024]{3,1,2,0:T(2,128)}, f32[1,2,128,1024]{3,1,2,0:T(2,128)}, u32[]{:S(2)}, u32[]{:S(2)}) collective-permute-start(f32[1,2,128,1024]{3,1,2,0:T(2,128)} %get-tuple-element.23), channel_id=1, source_target_pairs={{0,4},{4,8},{8,12},{12,16},{16,20},{20,24},{24,28},{28,32},{32,36}... | collective-permute-start | bytes 3145736 | tf_op jit(solution)/shard_map/ppermute | solution.py:16
  357.9 211.2 %collective-permute-start.8 = (f32[1,2,128,1024]{3,1,2,0:T(2,128)}, f32[1,2,128,1024]{3,1,2,0:T(2,128)}, u32[]{:S(2)}, u32[]{:S(2)}) collective-permute-start(f32[1,2,128,1024]{3,1,2,0:T(2,128)} %get-tuple-element.24), channel_id=1, source_target_pairs={{12,0},{16,4},{20,8},{24,12},{28,16},{32,20},{36,24},{40,28},{44,3... | collective-permute-start | bytes 3145736 | tf_op jit(solution)/shard_map/ppermute | solution.py:16
  388.9 180.3 %collective-permute-start.6 = (f32[1,2,128,1024]{3,1,2,0:T(2,128)}, f32[1,2,128,1024]{3,1,2,0:T(2,128)}, u32[]{:S(2)}, u32[]{:S(2)}) collective-permute-start(f32[1,2,128,1024]{3,1,2,0:T(2,128)} %get-tuple-element.25), channel_id=1, source_target_pairs={{4,0},{8,4},{12,8},{16,12},{20,16},{24,20},{28,24},{32,28},{36,32}... | collective-permute-start | bytes 3145736 | tf_op jit(solution)/shard_map/ppermute | solution.py:16
  391.1 175.4 %copy-start.27 = (f32[2]{0:T(128)S(1)}, f32[2]{0:T(128)}, u32[]{:S(2)}) copy-start(f32[2]{0:T(128)} %compare_convert_fusion) | copy-start | bytes 28
  392.7 176.5 %copy-start.22 = (f32[1,2,128,1024]{3,1,2,0:T(2,128)S(1)}, f32[1,2,128,1024]{3,1,2,0:T(2,128)}, u32[]{:S(2)}) copy-start(f32[1,2,128,1024]{3,1,2,0:T(2,128)} %copy-done.21) | copy-start | bytes 3145732
  (14 other events, 55.1 us)
Sparse Core Ops, SparseCore 0:
  25.1 197.4 all-reduce.7
  330.3 236.2 all-reduce.5
where the time goes:
time: 595 us; the launch traced here: 588 us
  waiting for transfers between devices  267 us (45%)
  blocking collectives  95.3 us (16%)
  matrix products  71.3 us (12%)
  local copies, waits for them, and re-layouts  70.5 us (12%)
  other arithmetic  34.4 us (6%)
  starting transfers between devices  34.1 us (6%)
  between operations  15.7 us (3%)
    psum x1, waiting for transfers between devices, broadcast(): return lax.psum(kept, axis)  163 us
    psum x1, blocking collectives, body(): bias_total = lax.psum(local_bias, ('ctx', 'dp'))  95.3 us
    psum x1, waiting for transfers between devices, body(): shared_total = lax.psum(prompt_grad, 'ctx')  75.6 us
    ppermute x12, starting transfers between devices, from_behind(): lax.ppermute(value, axis, [(source, source + steps) for source in range(i...  34 us
    ppermute x12, waiting for transfers between devices, from_behind(): lax.ppermute(value, axis, [(source, source + steps) for source in range(i...  28.9 us
    dot_general x2, matrix products, body(): jnp.einsum('dn,tdbf->tnbf', chooser[half_idx].astype(jnp.float32), contri...  17.5 us
    unnamed x69, local copies, waits for them, and re-layouts  14.9 us
    dot_general x2, matrix products, attend(): jnp.einsum('tqkgd,tskd->tkgqs', grad_rows, cand_vals, preferred_element_t...  14.4 us
  transfers between devices with their start and end apart: 14, of which 5 were waited for; matrix products, arithmetic and copies ran while one was open for 9% of the time, Pallas kernels for 0%

commit v1 on v0

--- a/solution.py
+++ b/solution.py
@@ -179,7 +179,7 @@
     query_all = jnp.stack(query_parts, axis=1)
     local_bias = jnp.sum(query_all, axis=(0, 1, 2)).reshape(width_q)
     shared_total = lax.psum(prompt_grad, "ctx")
-    bias_total = lax.psum(local_bias, ("ctx", "dp"))
+    bias_total = lax.psum(lax.psum(local_bias, "dp"), "ctx")
     owned = (owners == rank_ctx).astype(jnp.float32)
     kv_grad = kv_grad.at[:, 0].add(jnp.sum(owned[None, :, None, None] * shared_total, axis=1))
     grad_query_out = query_all.reshape(traces, 2 * BLOCK, width_q).astype(jnp.bfloat16)

time: 595 us -> 687 us (1.15)
  blocking collectives: 95.3 us -> 260 us
  waiting for transfers between devices: 267 us -> 191 us
    psum x1 -> x2, blocking collectives: 95.3 us -> 260 us  [body(): bias_total = lax.psum(lax.psum(local_bias, 'dp'), 'ctx')]
    psum x1, waiting for transfers between devices: 75.6 us -> 0.01 us  [body(): shared_total = lax.psum(prompt_grad, 'ctx')]
  transfers between devices with their start and end apart: 14 -> 14, of which waited for: 5 -> 4; matrix products, arithmetic and copies ran while one was open for 9% -> 8% of each run, Pallas kernels for 0% -> 0%
where the time goes in v1:
time: 687 us; the launch traced here: 677 us
  blocking collectives  260 us (38%)
  waiting for transfers between devices  191 us (28%)
  matrix products  71.3 us (10%)
  local copies, waits for them, and re-layouts  70.6 us (10%)
  other arithmetic  34.3 us (5%)
  starting transfers between devices  34.1 us (5%)
  between operations  15.7 us (2%)
    psum x2, blocking collectives, body(): bias_total = lax.psum(lax.psum(local_bias, 'dp'), 'ctx')  260 us
    psum x1, waiting for transfers between devices, broadcast(): return lax.psum(kept, axis)  163 us
    ppermute x12, starting transfers between devices, from_behind(): lax.ppermute(value, axis, [(source, source + steps) for source in range(i...  34 us
    ppermute x12, waiting for transfers between devices, from_behind(): lax.ppermute(value, axis, [(source, source + steps) for source in range(i...  28.9 us
    dot_general x2, matrix products, body(): jnp.einsum('dn,tdbf->tnbf', chooser[half_idx].astype(jnp.float32), contri...  17.5 us
    unnamed x69, local copies, waits for them, and re-layouts  14.9 us
    dot_general x2, matrix products, attend(): jnp.einsum('tqkgd,tskd->tkgqs', grad_rows, cand_vals, preferred_element_t...  14.4 us
  transfers between devices with their start and end apart: 14, of which 4 were waited for; matrix products, arithmetic and copies ran while one was open for 8% of the time, Pallas kernels for 0%

profile of v1, /device:TPU:2, one launch (start us, length us, event | category | flops | bytes accessed | tf_op | source)
XLA Modules:
  0.0 677.1 jit_solution(3771687152625029068)
XLA Ops:
  9.7 4.2 collective-permute-start.4
  15.9 4.8 collective-permute-start.2
  35.2 2.9 fusion.73
  38.3 3.7 collective-permute-start
  42.5 3.3 fusion.74
  48.8 4.5 collective-permute-done
  55.6 2.7 convert_bitcast_fusion
  60.0 162.5 %all-reduce.8.cloned.1.call-done = (bf16[1,1,128,1024]{3,1,2,0:T(2,128)(2,1)}, bf16[1,1,128,1024]{3,1,2,0:T(2,128)(2,1)}) async-done(((bf16[1,1,128,1024]{3,1,2,0:T(2,128)(2,1)}, bf16[1,1,128,1024]{3,1,2,0:T(2,128)(2,1)}), (bf16[1,1,128,1024]{3,1,2,0:T(2,128)(2,1)}, bf16[1,1,128,1024]{3,1,2,0:T(2,128)(2,1)})) %all-reduce.8.cloned.1.call-update) | async-done | bytes 524304 | tf_op jit(solution)/shard_map/psum | solution.py:21
  222.6 4.6 pad_maximum_fusion
  233.6 2.7 fusion.75
  248.8 3.2 fusion.9
  252.1 5.3 fusion.40
  257.4 5.2 fusion.29
  262.6 7.1 %fusion.11 = bf16[4,8,128,768]{2,3,1,0:T(8,128)(2,1)S(1)} fusion(f32[4,8,128]{2,1,0:T(8,128)S(1)} %bitcast.338, f32[4,8,128]{2,1,0:T(8,128)S(1)} %broadcast_select_fusion.2, f32[4,8,128]{2,1,0:T(8,128)S(1)} %get-tuple-element.46, f32[4,768,128,8]{2,1,3,0:T(8,128)S(1)} %get-tuple-element.47, pred[128,768]{0,1:T(8,128)(4,1)S(1)} %and_and_fusion, ...), kind=kOutput, calls=%fused_computation.19 | convolution fusion | flops 830472192 | bytes 20856832 | tf_op jit(solution)/shard_map/tqkgd,tskd->tkgqs/dot_general | solution.py:41
  272.8 3.4 fusion.35
  276.2 2.8 copy.106
  279.1 3.8 copy_dynamic-update-slice_fusion.1
  285.2 3.2 fusion.7
  288.5 4.8 fusion.37
  293.3 5.2 fusion.30
  298.5 7.3 %fusion.10 = bf16[4,8,128,768]{2,3,1,0:T(8,128)(2,1)S(1)} fusion(f32[4,8,128]{2,1,0:T(8,128)S(1)} %bitcast.339, f32[4,8,128]{2,1,0:T(8,128)S(1)} %broadcast_select_fusion.3, f32[4,8,128]{2,1,0:T(8,128)S(1)} %get-tuple-element.48, f32[4,768,128,8]{2,1,3,0:T(8,128)S(1)} %get-tuple-element.49, pred[128,768]{0,1:T(8,128)(4,1)S(1)} %and_and_fusion.1, ...), kind=kOutput, calls=%fused_computation.18 | convolution fusion | flops 830472192 | bytes 20856832 | tf_op jit(solution)/shard_map/tqkgd,tskd->tkgqs/dot_general | solution.py:41
  308.9 3.4 fusion.36
  318.4 6.9 %fusion.28 = f32[128,1024,14]{1,2,0:T(8,128)} fusion(f32[1,6,128,1024]{3,1,2,0:T(8,128)S(1)} %copy_dynamic-update-slice_fusion.2, pred[2,4,14]{2,1,0:T(4,128)(4,1)S(1)} %copy-done.26), kind=kOutput, calls=%fused_computation.40 | convolution fusion | flops 88080384 | bytes 9437696 | tf_op jit(solution)/shard_map/dn,tdbf->tnbf/dot_general | solution.py:154
  330.3 10.6 %add_bitcast_fusion = f32[1,14,128,1024]{3,1,2,0:T(8,128)S(1)} fusion(f32[128,1024,14]{1,2,0:T(8,128)} %fusion.28, f32[1,6,128,1024]{3,1,2,0:T(8,128)} %copy-done.4, pred[2,4,14]{2,1,0:T(4,128)(4,1)S(1)} %copy-done.26), kind=kOutput, calls=%fused_computation.17 | convolution fusion | flops 89915392 | bytes 17826304 | tf_op jit(solution)/shard_map/dn,tdbf->tnbf/dot_general | solution.py:154
  341.0 3.6 fusion.71
  350.6 3.0 collective-permute-start.10
  353.6 4.5 collective-permute-start.9
  365.3 23.8 %collective-permute-done.7 = f32[1,2,128,1024]{3,1,2,0:T(2,128)S(1)} collective-permute-done((f32[1,2,128,1024]{3,1,2,0:T(2,128)S(1)}, f32[1,2,128,1024]{3,1,2,0:T(2,128)S(1)}, u32[]{:S(2)}, u32[]{:S(2)}) %collective-permute-start.7) | collective-permute-done | bytes 1048608 | tf_op jit(solution)/shard_map/ppermute | solution.py:16
  395.2 16.9 %psum.38 = f32[4096]{0:T(1024)S(1)} all-reduce(f32[4096]{0:T(1024)S(1)} %add_bitcast_fusion.1), channel_id=1, replica_groups=mesh['ctx'=64,'dp'=4] {'dp'}, use_global_device_ids=true, to_apply=%region_14.15 | all-reduce | flops 4096 | bytes 32768 | tf_op jit(solution)/shard_map/psum | solution.py:182
  412.0 242.7 %psum.39 = f32[4096]{0:T(1024)S(1)} all-reduce(f32[4096]{0:T(1024)S(1)} %psum.38), channel_id=1, replica_groups=mesh['ctx'=64,'dp'=4] {'ctx'}, use_global_device_ids=true, to_apply=%region_15.16 | all-reduce | flops 4096 | bytes 32768 | tf_op jit(solution)/shard_map/psum | solution.py:182
  658.0 5.5 fusion.45
  664.1 3.7 scatter-add.4
  (171 shorter events, 89.6 us)
Async XLA Ops:
  7.2 20.2 %copy-start.13 = (bf16[1,256,4096]{2,1,0:T(8,128)(2,1)S(1)}, bf16[1,256,4096]{2,1,0:T(8,128)(2,1)}, u32[]{:S(2)}) copy-start(bf16[1,256,4096]{2,1,0:T(8,128)(2,1)} %param.9) | copy-start | bytes 6291460
  7.2 215.4 %all-reduce.8.cloned.1.call-start = ((), (), s32[]{:S(2)}) async-start(), calls=%async_computation.1 | async-start | bytes 2097152 | tf_op jit(solution)/shard_map/psum | solution.py:21
  8.4 29.9 %collective-permute-start.5 = (bf16[1,2,128,1024]{3,2,1,0:T(8,128)(2,1)S(1)}, bf16[1,2,128,1024]{3,2,1,0:T(8,128)(2,1)}, u32[]{:S(2)}, u32[]{:S(2)}) collective-permute-start(bf16[1,2,128,1024]{3,2,1,0:T(8,128)(2,1)S(1)} %bitcast.327), channel_id=1, source_target_pairs={{12,0},{16,4},{20,8},{24,12},{28,16},{32,20},{36,24},{40,28},{44,3... | collective-permute-start | bytes 1572872 | tf_op jit(solution)/shard_map/ppermute | solution.py:16
  9.7 36.0 %collective-permute-start.4 = (bf16[1,2,128,1024]{3,2,1,0:T(8,128)(2,1)S(1)}, bf16[1,2,128,1024]{3,2,1,0:T(8,128)(2,1)}, u32[]{:S(2)}, u32[]{:S(2)}) collective-permute-start(bf16[1,2,128,1024]{3,2,1,0:T(8,128)(2,1)S(1)} %bitcast.328), channel_id=1, source_target_pairs={{8,0},{12,4},{16,8},{20,12},{24,16},{28,20},{32,24},{36,28},{40,32... | collective-permute-start | bytes 1572872 | tf_op jit(solution)/shard_map/ppermute | solution.py:16
  13.9 31.8 %collective-permute-start.3 = (bf16[1,2,128,1024]{3,2,1,0:T(8,128)(2,1)S(1)}, bf16[1,2,128,1024]{3,2,1,0:T(8,128)(2,1)}, u32[]{:S(2)}, u32[]{:S(2)}) collective-permute-start(bf16[1,2,128,1024]{3,2,1,0:T(8,128)(2,1)S(1)} %bitcast.329), channel_id=1, source_target_pairs={{4,0},{8,4},{12,8},{16,12},{20,16},{24,20},{28,24},{32,28},{36,32}... | collective-permute-start | bytes 1572872 | tf_op jit(solution)/shard_map/ppermute | solution.py:16
  15.9 32.3 %collective-permute-start.2 = (bf16[1,2,128,1024]{3,2,1,0:T(8,128)(2,1)S(1)}, bf16[1,2,128,1024]{3,2,1,0:T(8,128)(2,1)}, u32[]{:S(2)}, u32[]{:S(2)}) collective-permute-start(bf16[1,2,128,1024]{3,2,1,0:T(8,128)(2,1)S(1)} %bitcast.330), channel_id=1, source_target_pairs={{0,12},{4,16},{8,20},{12,24},{16,28},{20,32},{24,36},{28,40},{32,4... | collective-permute-start | bytes 1572872 | tf_op jit(solution)/shard_map/ppermute | solution.py:16
  20.7 28.1 %collective-permute-start.1 = (bf16[1,2,128,1024]{3,2,1,0:T(8,128)(2,1)S(1)}, bf16[1,2,128,1024]{3,2,1,0:T(8,128)(2,1)}, u32[]{:S(2)}, u32[]{:S(2)}) collective-permute-start(bf16[1,2,128,1024]{3,2,1,0:T(8,128)(2,1)S(1)} %bitcast.331), channel_id=1, source_target_pairs={{0,8},{4,12},{8,16},{12,20},{16,24},{20,28},{24,32},{28,36},{32,40... | collective-permute-start | bytes 1572872 | tf_op jit(solution)/shard_map/ppermute | solution.py:16
  25.0 630.4 %all-reduce.6.cloned.1.call-start = ((), (), s32[]{:S(2)}) async-start(), calls=%async_computation | async-start | bytes 2097152 | tf_op jit(solution)/shard_map/psum | solution.py:181
  32.8 22.8 %copy-start.25 = (pred[2,4,14]{2,1,0:T(4,128)(4,1)}, pred[2,4,14]{2,1,0:T(4,128)(4,1)S(1)}, u32[]{:S(2)}) copy-start(pred[2,4,14]{2,1,0:T(4,128)(4,1)S(1)} %broadcast_compare_fusion.2) | copy-start | bytes 340
  38.1 208.3 %copy-start.9 = (bf16[1,1,128,4,8,128]{5,4,3,2,1,0:T(8,128)(2,1)}, bf16[1,1,128,4,8,128]{5,4,3,2,1,0:T(8,128)(2,1)S(1)}, u32[]{:S(2)}) copy-start(bf16[1,1,128,4,8,128]{5,4,3,2,1,0:T(8,128)(2,1)S(1)} %get-tuple-element.29) | copy-start | bytes 3145732
  38.3 15.0 %collective-permute-start = (bf16[1,2,128,1024]{3,2,1,0:T(8,128)(2,1)S(1)}, bf16[1,2,128,1024]{3,2,1,0:T(8,128)(2,1)S(1)}, u32[]{:S(2)}, u32[]{:S(2)}) collective-permute-start(bf16[1,2,128,1024]{3,2,1,0:T(8,128)(2,1)S(1)} %bitcast.333), channel_id=1, source_target_pairs={{0,4},{4,8},{8,12},{12,16},{16,20},{20,24},{24,28},{28,32},{32,36}... | collective-permute-start | bytes 1572872 | tf_op jit(solution)/shard_map/ppermute | solution.py:16
  239.1 9.7 %copy-start.5 = (bf16[768,4,128]{2,1,0:T(4,128)(2,1)}, bf16[768,4,128]{2,1,0:T(4,128)(2,1)S(1)}, u32[]{:S(2)}) copy-start(bf16[768,4,128]{2,1,0:T(4,128)(2,1)S(1)} %reshape.1055) | copy-start | bytes 2359300
  252.1 5.3 copy-start.24
  262.6 7.1 %copy-start.15 = (f32[1,768,4,128]{3,1,2,0:T(8,128)S(1)}, f32[1,768,4,128]{3,1,2,0:T(8,128)}, u32[]{:S(2)}) copy-start(f32[1,768,4,128]{3,1,2,0:T(8,128)} %fusion.40) | copy-start | bytes 4718596
  262.6 10.2 %copy-start.10 = (bf16[1,1,128,4,8,128]{5,4,3,2,1,0:T(8,128)(2,1)S(1)}, bf16[1,1,128,4,8,128]{5,4,3,2,1,0:T(8,128)(2,1)}, u32[]{:S(2)}) copy-start(bf16[1,1,128,4,8,128]{5,4,3,2,1,0:T(8,128)(2,1)} %copy-done.9) | copy-start | bytes 3145732
  276.2 6.6 copy-start.7
  298.5 7.3 %copy-start.16 = (f32[1,768,4,128]{3,1,2,0:T(8,128)S(1)}, f32[1,768,4,128]{3,1,2,0:T(8,128)}, u32[]{:S(2)}) copy-start(f32[1,768,4,128]{3,1,2,0:T(8,128)} %fusion.37) | copy-start | bytes 4718596
  298.5 10.5 %copy-start.8 = (bf16[1,1,128,4,8,128]{5,4,3,2,1,0:T(8,128)(2,1)S(1)}, bf16[1,1,128,4,8,128]{5,4,3,2,1,0:T(8,128)(2,1)}, u32[]{:S(2)}) copy-start(bf16[1,1,128,4,8,128]{5,4,3,2,1,0:T(8,128)(2,1)} %get-tuple-element.28) | copy-start | bytes 3145732
  312.3 6.0 copy-start.26
  318.3 6.9 %copy-start.3 = (f32[1,6,128,1024]{3,1,2,0:T(8,128)S(1)}, f32[1,6,128,1024]{3,1,2,0:T(8,128)}, u32[]{:S(2)}) copy-start(f32[1,6,128,1024]{3,1,2,0:T(8,128)} %copy_dynamic-update-slice_fusion.1) | copy-start | bytes 9437188
  318.4 6.9 %copy-start.11 = (f32[1,768,4,128]{3,2,0,1:T(4,128)S(1)}, f32[1,768,4,128]{3,2,0,1:T(4,128)}, u32[]{:S(2)}) copy-start(f32[1,768,4,128]{3,2,0,1:T(4,128)} %copy.107) | copy-start | bytes 4718596
  328.3 31.9 %slice-start = ((s8[6291456]{0:T(1024)(128)(4,1)}), s8[2097152]{0:T(1024)(128)(4,1)S(1)}, s32[]{:S(2)}) async-start(s8[6291456]{0:T(1024)(128)(4,1)} %bitcast.308), calls=%async_computation.2 | async-start | bytes 4194304
  330.3 29.8 %slice-start.1 = ((s8[6291456]{0:T(1024)(128)(4,1)}), s8[4194304]{0:T(1024)(128)(4,1)S(1)}, s32[]{:S(2)}) async-start(s8[6291456]{0:T(1024)(128)(4,1)} %bitcast.308), calls=%async_computation.3 | async-start | bytes 8388608
  341.0 19.2 %copy-start.6 = (bf16[768,4,128]{2,1,0:T(4,128)(2,1)S(1)}, bf16[768,4,128]{2,1,0:T(4,128)(2,1)}, u32[]{:S(2)}) copy-start(bf16[768,4,128]{2,1,0:T(4,128)(2,1)} %copy-done.5) | copy-start | bytes 2359300
  345.8 43.2 %collective-permute-start.7 = (f32[1,2,128,1024]{3,1,2,0:T(2,128)S(1)}, f32[1,2,128,1024]{3,1,2,0:T(2,128)S(1)}, u32[]{:S(2)}, u32[]{:S(2)}) collective-permute-start(f32[1,2,128,1024]{3,1,2,0:T(2,128)S(1)} %get-tuple-element.20), channel_id=1, source_target_pairs={{8,0},{12,4},{16,8},{20,12},{24,16},{28,20},{32,24},{36,28},{40,32... | collective-permute-start | bytes 3145736 | tf_op jit(solution)/shard_map/ppermute | solution.py:16
  348.3 309.7 %collective-permute-start.11 = (f32[1,2,128,1024]{3,1,2,0:T(2,128)}, f32[1,2,128,1024]{3,1,2,0:T(2,128)}, u32[]{:S(2)}, u32[]{:S(2)}) collective-permute-start(f32[1,2,128,1024]{3,1,2,0:T(2,128)} %get-tuple-element.21), channel_id=1, source_target_pairs={{0,12},{4,16},{8,20},{12,24},{16,28},{20,32},{24,36},{28,40},{32,4... | collective-permute-start | bytes 3145736 | tf_op jit(solution)/shard_map/ppermute | solution.py:16
  350.6 307.4 %collective-permute-start.10 = (f32[1,2,128,1024]{3,1,2,0:T(2,128)}, f32[1,2,128,1024]{3,1,2,0:T(2,128)}, u32[]{:S(2)}, u32[]{:S(2)}) collective-permute-start(f32[1,2,128,1024]{3,1,2,0:T(2,128)} %get-tuple-element.22), channel_id=1, source_target_pairs={{0,8},{4,12},{8,16},{12,20},{16,24},{20,28},{24,32},{28,36},{32,40... | collective-permute-start | bytes 3145736 | tf_op jit(solution)/shard_map/ppermute | solution.py:16
  353.6 304.4 %collective-permute-start.9 = (f32[1,2,128,1024]{3,1,2,0:T(2,128)}, f32[1,2,128,1024]{3,1,2,0:T(2,128)}, u32[]{:S(2)}, u32[]{:S(2)}) collective-permute-start(f32[1,2,128,1024]{3,1,2,0:T(2,128)} %get-tuple-element.23), channel_id=1, source_target_pairs={{0,4},{4,8},{8,12},{12,16},{16,20},{20,24},{24,28},{28,32},{32,36}... | collective-permute-start | bytes 3145736 | tf_op jit(solution)/shard_map/ppermute | solution.py:16
  358.1 299.9 %collective-permute-start.8 = (f32[1,2,128,1024]{3,1,2,0:T(2,128)}, f32[1,2,128,1024]{3,1,2,0:T(2,128)}, u32[]{:S(2)}, u32[]{:S(2)}) collective-permute-start(f32[1,2,128,1024]{3,1,2,0:T(2,128)} %get-tuple-element.24), channel_id=1, source_target_pairs={{12,0},{16,4},{20,8},{24,12},{28,16},{32,20},{36,24},{40,28},{44,3... | collective-permute-start | bytes 3145736 | tf_op jit(solution)/shard_map/ppermute | solution.py:16
  389.0 269.0 %collective-permute-start.6 = (f32[1,2,128,1024]{3,1,2,0:T(2,128)}, f32[1,2,128,1024]{3,1,2,0:T(2,128)}, u32[]{:S(2)}, u32[]{:S(2)}) collective-permute-start(f32[1,2,128,1024]{3,1,2,0:T(2,128)} %get-tuple-element.25), channel_id=1, source_target_pairs={{4,0},{8,4},{12,8},{16,12},{20,16},{24,20},{28,24},{32,28},{36,32}... | collective-permute-start | bytes 3145736 | tf_op jit(solution)/shard_map/ppermute | solution.py:16
  391.3 264.1 %copy-start.27 = (f32[2]{0:T(128)S(1)}, f32[2]{0:T(128)}, u32[]{:S(2)}) copy-start(f32[2]{0:T(128)} %compare_convert_fusion) | copy-start | bytes 28
  392.8 265.2 %copy-start.22 = (f32[1,2,128,1024]{3,1,2,0:T(2,128)S(1)}, f32[1,2,128,1024]{3,1,2,0:T(2,128)}, u32[]{:S(2)}) copy-start(f32[1,2,128,1024]{3,1,2,0:T(2,128)} %copy-done.21) | copy-start | bytes 3145732
  (14 other events, 55.1 us)
Sparse Core Ops, SparseCore 0:
  25.1 197.4 all-reduce.7
  330.4 237.1 all-reduce.5
